TPU v7x, 256 devices: a whole 4x4x8 slice. The times are simulated.
256 devices in a mesh: blk: 32 (over z, y_hi, core), head: 8 (over x, y_lo).
Axes of the slice: x: 4, y: 4 (y_hi: 2, y_lo: 2; y = y_hi * 2 + y_lo), z: 8, core: 2. Of those that a mesh axis runs over, the one named last changes fastest.
Arguments:
- query_nope: bfloat16 [2048, 16384], P('blk', 'head'), may hold values from -6 to 6
- query_rope: bfloat16 [2048, 8192], P('blk', 'head'), may hold values from -16 to 16
- key_absorb: bfloat16 [128, 128, 512], P('head'), may hold values from -0.5 to 0.5
- value_absorb: bfloat16 [128, 512, 128], P('head'), may hold values from -0.25 to 0.25
- out_weight: bfloat16 [16384, 7168], P('head', 'blk'), may hold values from -0.046875 to 0.046875
- latent_cache: bfloat16 [512, 4096], P(None, 'blk'), may hold values from -9 to 9
- rope_key: bfloat16 [64, 4096], P(None, 'blk'), may hold values from -6 to 6
Outputs:
- answers: bfloat16 [2048, 7168], P('head', 'blk')
All inputs are finite; a program needn't handle non-finite values.
Results may differ from a plain program's by a relative error of at most 0.019.
Values may be sent and summed in bfloat16 or wider, within the bound.
A program may use at most 128 MiB of HBM per device.

v0:
```python
import jax
import jax.numpy as jnp
from jax import lax
from jax.sharding import PartitionSpec as P


def body(query_nope, query_rope, key_absorb, value_absorb, out_weight, latent_cache, rope_key):
    query_rows = query_nope.shape[0]
    head_count = key_absorb.shape[0]
    queries = jnp.einsum(
        "qhd,hdc->qhc",
        query_nope.reshape(query_rows, head_count, key_absorb.shape[1]),
        key_absorb,
        preferred_element_type=jnp.float32,
    ).astype(jnp.bfloat16)
    rotary = query_rope.reshape(query_rows, head_count, rope_key.shape[0])
    score_scale = (key_absorb.shape[1] + rope_key.shape[0]) ** (-0.5)
    running_max = jnp.full((query_rows, head_count), -1e30, jnp.float32)
    latent_piece = lax.all_gather(latent_cache, "blk", axis=1, tiled=True)
    rotary_piece = lax.all_gather(rope_key, "blk", axis=1, tiled=True)
    scores = (
        jnp.einsum("qhc,cn->qhn", queries, latent_piece, preferred_element_type=jnp.float32)
        + jnp.einsum("qhr,rn->qhn", rotary, rotary_piece, preferred_element_type=jnp.float32)
    ) * score_scale
    new_max = jnp.maximum(running_max, jnp.max(scores, axis=-1))
    weights = jnp.exp(scores - new_max[..., None])
    running_sum = jnp.sum(weights, axis=-1)
    weighted = jnp.einsum(
        "qhn,cn->qhc",
        weights.astype(jnp.bfloat16),
        latent_piece,
        preferred_element_type=jnp.float32,
    )
    mixture = (weighted / running_sum[..., None]).astype(jnp.bfloat16)
    attended = jnp.einsum(
        "qhc,hcv->qhv", mixture, value_absorb, preferred_element_type=jnp.float32
    ).astype(jnp.bfloat16)
    attended = attended.reshape(query_rows, head_count * value_absorb.shape[2])
    partials = jnp.dot(
        lax.all_gather(attended, "blk", axis=0, tiled=True),
        out_weight,
        preferred_element_type=jnp.float32,
    )
    return lax.psum_scatter(partials.astype(jnp.bfloat16), "head", scatter_dimension=0, tiled=True)


def solution(mesh):
    in_specs = (
        P("blk", "head"),
        P("blk", "head"),
        P("head", None, None),
        P("head", None, None),
        P("head", "blk"),
        P(None, "blk"),
        P(None, "blk"),
    )
    out_specs = P("head", "blk")
    return jax.shard_map(body, mesh=mesh, in_specs=in_specs, out_specs=out_specs, check_vma=False)
```

profile of v0, /device:TPU:32, one launch (start us, length us, event | category | flops | bytes accessed | tf_op | source)
XLA Modules:
  0.0 286.2 jit_solution(3412229803459003356)
XLA Ops:
  6.5 0.0 copy-start
  6.5 0.0 all-gather.3.cloned.1.call-start
  6.5 0.7 all-gather.3.cloned.1.call-update
  7.3 0.0 all-gather.5.cloned.1.call-start
  7.3 1.1 reshape.14
  8.4 44.1 %all_gather.10 = bf16[64,4096]{1,0:T(8,128)(2,1)S(1)} all-gather(bf16[64,128]{1,0:T(8,128)(2,1)} %param.13), channel_id=1, replica_groups=mesh['blk'=32,'head'=8] {'blk'}, dimensions={1}, use_global_device_ids=true | all-gather | bytes 540672 | tf_op jit(solution)/shard_map/all_gather | solution.py:20
  52.6 0.0 copy-done
  52.6 2.3 fusion.12
  54.9 45.6 %all-gather.3.cloned.1.call-done = bf16[512,4096]{1,0:T(8,128)(2,1)} async-done(((bf16[512,128]{1,0:T(8,128)(2,1)}), bf16[512,4096]{1,0:T(8,128)(2,1)}) %all-gather.3.cloned.1.call-update) | async-done | bytes 4194320 | tf_op jit(solution)/shard_map/all_gather | solution.py:19
  100.5 6.9 %fusion.6 = f32[64,16,4096]{2,1,0:T(8,128)S(1)} fusion(bf16[512,4096]{1,0:T(8,128)(2,1)} %all-gather.3.cloned.1.call-done, bf16[64,16,512]{2,0,1:T(8,128)(2,1)} %fusion.12), kind=kOutput, calls=%fused_computation.7 | convolution fusion | flops 4294967296 | bytes 22020096 | tf_op jit(solution)/shard_map/qhc,cn->qhn/dot_general | solution.py:22
  107.4 7.1 %fusion.19 = (f32[64,16]{1,0:T(8,128)S(1)}, f32[64,16,4096]{2,1,0:T(8,128)}) fusion(f32[64,16,4096]{2,1,0:T(8,128)S(1)} %fusion.6, bf16[64,16,64]{2,1,0:T(8,128)(2,1)S(1)} %reshape.14, bf16[64,4096]{1,0:T(8,128)(2,1)S(1)} %all_gather.10), kind=kOutput, calls=%fused_computation.22 | convolution fusion | flops 549452800 | bytes 34213888 | tf_op jit(solution)/shard_map/qhr,rn->qhn/dot_general | solution.py:23
  114.5 8.1 %fusion = f32[64,16]{1,0:T(8,128)S(1)} fusion(f32[64,16,4096]{2,1,0:T(8,128)} %get-tuple-element.6, f32[64,16]{1,0:T(8,128)S(1)} %broadcast_maximum_fusion), kind=kLoop, calls=%fused_computation.2 | loop fusion | flops 8387584 | bytes 16785408 | tf_op jit(solution)/shard_map/reduce_sum | solution.py:27
  122.6 0.0 copy-start.1
  122.6 0.0 copy-start.2
  122.6 11.7 %divide_convert_fusion = bf16[64,16,512]{2,1,0:T(8,128)(2,1)S(1)} fusion(bf16[512,4096]{1,0:T(8,128)(2,1)} %all-gather.3.cloned.1.call-done, f32[64,16,4096]{2,1,0:T(8,128)} %get-tuple-element.6, f32[64,16]{1,0:T(8,128)S(1)} %broadcast_maximum_fusion, f32[64,16]{1,0:T(8,128)S(1)} %fusion), kind=kOutput, calls=%fused_computation.10 | convolution fusion | flops 4304404480 | bytes 22028288 | tf_op jit(solution)/shard_map/qhn,cn->qhc/dot_general | solution.py:28
  134.3 0.0 copy-done.1
  134.3 1.3 fusion.13
  135.6 0.8 copy.24
  136.4 0.0 all-gather.5.cloned.1.call-update
  136.4 0.0 reduce-scatter.2.cloned.1.call-start
  136.5 97.9 %all-gather.5.cloned.1.call-done = bf16[2048,2048]{1,0:T(8,128)(2,1)} async-done(((bf16[64,2048]{1,0:T(8,128)(2,1)}), bf16[2048,2048]{1,0:T(8,128)(2,1)}) %all-gather.5.cloned.1.call-update) | async-done | bytes 8388624 | tf_op jit(solution)/shard_map/all_gather | solution.py:40
  234.4 0.0 copy-done.2
  234.4 7.0 %convolution_convert_fusion = bf16[2048,224]{0,1:T(8,128)(2,1)} fusion(bf16[2048,2048]{1,0:T(8,128)(2,1)} %all-gather.5.cloned.1.call-done, bf16[2048,224]{0,1:T(8,128)(2,1)S(1)} %copy-done.2), kind=kOutput, calls=%fused_computation.9 | convolution fusion | flops 1879506944 | bytes 10223616 | tf_op jit(solution)/shard_map/dot_general | solution.py:39
  241.4 0.0 reduce-scatter.2.cloned.1.call-update
  241.5 38.2 %reduce-scatter.2.cloned.1.call-done = bf16[256,224]{0,1:T(8,128)(2,1)} async-done(((bf16[2048,224]{0,1:T(8,128)(2,1)}), bf16[256,224]{0,1:T(8,128)(2,1)}) %reduce-scatter.2.cloned.1.call-update) | async-done | bytes 114704 | tf_op jit(solution)/shard_map/reduce_scatter | solution.py:44
  (1 shorter events, 0.0 us)
Async XLA Ops:
  6.5 46.0 %copy-start = (bf16[16,128,512]{2,1,0:T(8,128)(2,1)S(1)}, bf16[16,128,512]{2,1,0:T(8,128)(2,1)}, u32[]{:S(2)}) copy-start(bf16[16,128,512]{2,1,0:T(8,128)(2,1)} %param.9) | copy-start | bytes 6291460
  6.5 94.0 %all-gather.3.cloned.1.call-start = ((), (), s32[]{:S(2)}) async-start(), calls=%async_computation.1 | async-start | bytes 4325376 | tf_op jit(solution)/shard_map/all_gather | solution.py:19
  7.3 227.2 %all-gather.5.cloned.1.call-start = ((), (), s32[]{:S(2)}) async-start(), calls=%async_computation.2 | async-start | bytes 8650752 | tf_op jit(solution)/shard_map/all_gather | solution.py:40
  122.6 11.7 %copy-start.1 = (bf16[16,512,128]{2,1,0:T(8,128)(2,1)S(1)}, bf16[16,512,128]{2,1,0:T(8,128)(2,1)}, u32[]{:S(2)}) copy-start(bf16[16,512,128]{2,1,0:T(8,128)(2,1)} %param.10) | copy-start | bytes 6291460
  122.6 111.8 %copy-start.2 = (bf16[2048,224]{0,1:T(8,128)(2,1)S(1)}, bf16[2048,224]{0,1:T(8,128)(2,1)}, u32[]{:S(2)}) copy-start(bf16[2048,224]{0,1:T(8,128)(2,1)} %param.11) | copy-start | bytes 2752516
  136.4 143.2 %reduce-scatter.2.cloned.1.call-start = ((), (), s32[]{:S(2)}) async-start(), calls=%async_computation.3 | async-start | bytes 1032192 | tf_op jit(solution)/shard_map/reduce_scatter | solution.py:44
Sparse Core Ops, SparseCore 0:
  9.9 90.5 all-gather.2
  136.5 97.8 all-gather.4
  241.6 38.0 reduce-scatter.1
where the time goes:
time: 286 us
  waiting for transfers between devices  183 us (64%)
  blocking collectives  44.1 us (15%)
  matrix products  36.3 us (13%)
  between operations  13.1 us (5%)
  other arithmetic  8.08 us (3%)
    all_gather x1, waiting for transfers between devices, body(): lax.all_gather(attended, 'blk', axis=0, tiled=True)  97.9 us
    all_gather x1, waiting for transfers between devices, body(): latent_piece = lax.all_gather(latent_cache, 'blk', axis=1, tiled=True)  45.6 us
    all_gather x1, blocking collectives, body(): rotary_piece = lax.all_gather(rope_key, 'blk', axis=1, tiled=True)  44.1 us
    reduce_scatter x1, waiting for transfers between devices, body(): lax.psum_scatter(partials.astype(jnp.bfloat16), 'head', scatter_dimension...  38.2 us
    dot_general x1, matrix products, body(): jnp.einsum('qhn,cn->qhc', weights.astype(jnp.bfloat16), latent_piece, pre...  11.7 us
    reduce_sum x1, other arithmetic, body(): running_sum = jnp.sum(weights, axis=-1)  8.07 us
    dot_general x1, matrix products, body(): jnp.einsum('qhr,rn->qhn', rotary, rotary_piece, preferred_element_type=jn...  7.06 us
    dot_general x1, matrix products, body(): jnp.dot(lax.all_gather(attended, 'blk', axis=0, tiled=True), out_weight,...  7.02 us
  transfers between devices with their start and end apart: 3, of which 3 were waited for; matrix products, arithmetic and copies ran while one was open for 1% of the time, Pallas kernels for 0%

commit v1 on v0

v1 whole, which is shorter than its diff:
```python
import functools
import math

import jax
import jax.numpy as jnp
from jax import lax
from jax.experimental import pallas as pl
from jax.experimental.pallas import tpu as pltpu
from jax.sharding import PartitionSpec as P

MESH = pl.DeviceIdType.MESH
F32 = jnp.float32
BF16 = jnp.bfloat16

Z = 8
X = 4
GROUPS = 4


def flip(value, bit):
    return value + bit - 2 * bit * (value // bit % 2)


def kernel(
    qn_hbm, qr_hbm, ka_hbm, va_hbm, w_hbm, lat_hbm, rk_hbm, out_ref,
    keys, queries, qn, qr, ka, va, weight, relay, scores, lane_max, lane_sum, acc,
    att, part, summed,
    local_sem, key_send, key_recv, w_send, w_recv, att_send, att_recv, out_send, out_recv,
):
    blk = lax.axis_index("blk")
    head = lax.axis_index("head")
    z = blk // 4
    mine = blk % 4
    yhi = mine // 2
    core = blk % 2
    x = head // 2
    sibling = flip(blk, 1)
    other_y = flip(blk, 2)
    head_y = flip(head, 1)
    side = 1 - 2 * core

    lat = lat_hbm.shape[0]
    rope = rk_hbm.shape[0]
    heads, nope = ka_hbm.shape[0], ka_hbm.shape[1]
    vd = va_hbm.shape[2]
    rows = qn_hbm.shape[0]
    pairs = heads * rows
    group_heads = heads // GROUPS
    group_rows = group_heads * rows
    factor = (nope + rope) ** (-0.5) * math.log2(math.e)

    def wrap_z(value):
        return (value + 2 * Z) % Z

    def at_z(step):
        return wrap_z(z + step) * 4 + mine

    def at_x(step):
        return (x + step + X) % X * 2 + head % 2

    loads = [
        pltpu.make_async_copy(lat_hbm, keys.at[blk, pl.ds(0, lat)], local_sem.at[0]),
        pltpu.make_async_copy(rk_hbm, keys.at[blk, pl.ds(lat, rope)], local_sem.at[1]),
        pltpu.make_async_copy(qn_hbm, qn, local_sem.at[2]),
        pltpu.make_async_copy(qr_hbm, qr, local_sem.at[3]),
        pltpu.make_async_copy(ka_hbm, ka, local_sem.at[4]),
        pltpu.make_async_copy(w_hbm, weight.at[mine], local_sem.at[5]),
        pltpu.make_async_copy(va_hbm, va, local_sem.at[6]),
    ]
    for load in loads:
        load.start()

    barrier = pltpu.get_barrier_semaphore()
    for step in (1, -1):
        pl.semaphore_signal(barrier, inc=1, device_id={"blk": at_z(step), "head": head}, device_id_type=MESH)

    def greet(i, carry):
        to_blk, to_head = z * 4 + i % 4, i // 4

        @pl.when(jnp.logical_or(to_blk != blk, to_head != head))
        def _():
            pl.semaphore_signal(barrier, inc=1, device_id={"blk": to_blk, "head": to_head}, device_id_type=MESH)

        return carry

    lax.fori_loop(0, 32, greet, 0)
    pl.semaphore_wait(barrier, 33)

    key_sends = []

    def key_copy(slot, to_blk, to_head):
        copy = pltpu.make_async_remote_copy(
            src_ref=keys.at[slot],
            dst_ref=keys.at[slot],
            send_sem=key_send.at[len(key_sends)],
            recv_sem=key_recv.at[slot],
            device_id={"blk": to_blk, "head": to_head},
            device_id_type=MESH,
        )
        key_sends.append(copy)
        return copy

    def key_wait(slot):
        pltpu.make_async_remote_copy(
            src_ref=keys.at[slot],
            dst_ref=keys.at[slot],
            send_sem=key_send.at[0],
            recv_sem=key_recv.at[slot],
            device_id={"blk": sibling, "head": head},
            device_id_type=MESH,
        ).wait_recv()

    def w_copy(index, src, dst, to_blk, to_head):
        return pltpu.make_async_remote_copy(
            src_ref=src,
            dst_ref=dst,
            send_sem=w_send.at[index],
            recv_sem=w_recv.at[index],
            device_id={"blk": to_blk, "head": to_head},
            device_id_type=MESH,
        )

    carried = (yhi + x) % 2

    def carry_slot(step):
        return wrap_z(z + step) * 4 + carried * 2 + core

    def other_slot(step):
        return wrap_z(z + step) * 4 + (1 - carried) * 2 + core

    loads[0].wait()
    loads[1].wait()
    key_copy(blk, other_y, head_y).start()
    first = [key_copy(carry_slot(0), at_z(1), head), key_copy(carry_slot(0), at_z(-1), head)]

    @pl.when(x % 2 == 0)
    def _():
        for copy in first:
            copy.start()

    key_copy(blk, sibling, head).start()

    lane_max[...] = jnp.full_like(lane_max, -jnp.inf)

    for index in (2, 3, 4):
        loads[index].wait()
    for h in range(heads):
        product = jnp.dot(qn[:, h * nope:(h + 1) * nope], ka[h], preferred_element_type=F32)
        queries[h * rows:(h + 1) * rows, 0:lat] = product.astype(BF16)
        queries[h * rows:(h + 1) * rows, lat:lat + rope] = qr[:, h * rope:(h + 1) * rope]

    half = weight.shape[1] // 2
    own_w = weight.at[mine]
    far = flip(mine, 2)
    loads[5].wait()
    w_sends = [
        w_copy(0, weight.at[mine, pl.ds(0, half)], relay.at[0], other_y, head_y),
        w_copy(1, weight.at[mine, pl.ds(half, half)], relay.at[1], blk, head_y),
        w_copy(2, own_w, own_w, sibling, head),
    ]
    for copy in w_sends:
        copy.start()

    key_wait(flip(blk, 2))

    @pl.when(x % 2 == 1)
    def _():
        for copy in first:
            copy.start()

    key_copy(flip(blk, 2), sibling, head).start()

    def unit(step, half_y):
        base = wrap_z(z + step) * 4 + half_y * 2
        block = jnp.concatenate([keys[base], keys[base + 1]], axis=1)
        product = jnp.dot(queries[...], block, preferred_element_type=F32)
        scores[base // 2] = product
        width = block.shape[1] // 2
        lane_max[...] = jnp.maximum(lane_max[...], jnp.maximum(product[:, :width], product[:, width:]))

    def own_units(i, carry):
        half_y = (yhi + i) % 2
        key_wait(z * 4 + half_y * 2 + 1 - core)
        unit(0, half_y)
        return carry

    lax.fori_loop(0, 2, own_units, 0)

    def units(count, carry_step, other_step):
        def one(i, carry):
            late = i // 2
            step = (1 - 2 * (i % 2)) * (carry_step + (other_step - carry_step) * late)
            half_y = (carried + late) % 2
            key_wait(wrap_z(z + step) * 4 + half_y * 2 + 1 - core)
            unit(step, half_y)
            return carry

        lax.fori_loop(0, count, one, 0)

    for step in (1, 2, 3):
        for way in (1, -1):
            slot = carry_slot(-way * step)
            key_wait(slot)
            if step < 3:
                key_copy(slot, at_z(way), head).start()
            key_copy(slot, blk, at_x(way)).start()
            key_copy(slot, sibling, head).start()
        if step == 3:
            key_copy(carry_slot(-side * 3), at_z(side), head).start()
        if step > 1:
            for way in (1, -1):
                slot = other_slot(-way * (step - 1))
                key_wait(slot)
                key_copy(slot, sibling, head).start()
            units(2 if step == 2 else 4, step - 1, step - 2)
    slot = carry_slot(4)
    key_wait(slot)
    key_copy(slot, blk, at_x(side)).start()
    key_copy(slot, sibling, head).start()

    w_sends[0].wait_recv()
    w_sends[1].wait_recv()
    w_sends.append(w_copy(3, relay.at[0], weight.at[far, pl.ds(0, half)], blk, head_y))
    w_sends.append(w_copy(4, relay.at[1], weight.at[mine, pl.ds(half, half)], other_y, head_y))
    w_sends[3].start()
    w_sends[4].start()

    for way in (1, -1):
        slot = other_slot(-way * 3)
        key_wait(slot)
        key_copy(slot, sibling, head).start()
    units(4, 3, 2)
    slot = other_slot(4)
    key_wait(slot)
    key_copy(slot, sibling, head).start()

    def late_units(i, carry):
        is_far = i // 2
        step = (1 - 2 * (i % 2)) * 3 * (1 - is_far) + 4 * is_far
        half_y = (carried + (1 - is_far) + is_far * (i % 2)) % 2
        key_wait(wrap_z(z + step) * 4 + half_y * 2 + 1 - core)
        unit(step, half_y)
        return carry

    lax.fori_loop(0, 4, late_units, 0)

    att_sends = {}

    def att_copy(index, slot, group, to_blk):
        return pltpu.make_async_remote_copy(
            src_ref=att.at[slot, group],
            dst_ref=att.at[slot, group],
            send_sem=att_send.at[index],
            recv_sem=att_recv.at[slot, group],
            device_id={"blk": to_blk, "head": head},
            device_id_type=MESH,
        )

    def att_forward(step, group, way):
        copy = att_copy(len(att_sends), wrap_z(z - way * step), group, at_z(way))
        copy.start()
        att_sends[step, group, way] = copy

    def att_wait(slot, group):
        att_copy(0, slot, group, at_z(1)).wait_recv()

    def pass_on(step, group):
        for way in (1, -1):
            att_wait(wrap_z(z - way * step), group)
            if step < 3 or (group % 2 == 0) == (way == 1):
                att_forward(step, group, way)

    loads[6].wait()
    for group in range(GROUPS):
        rows_at = pl.ds(group * group_rows, group_rows)
        top = jnp.max(lane_max[rows_at], axis=1, keepdims=True)
        acc[...] = jnp.zeros_like(acc)
        lane_sum[...] = jnp.zeros_like(lane_sum)

        def mix(i, carry):
            value = jnp.concatenate([scores[2 * i, rows_at], scores[2 * i + 1, rows_at]], axis=1)
            value = jnp.exp2((value - top) * factor)
            width = lane_sum.shape[1]
            total = value[:, 0:width]
            for k in range(1, value.shape[1] // width):
                total = total + value[:, k * width:(k + 1) * width]
            lane_sum[...] += total
            block = jnp.concatenate([keys[4 * i + k, 0:lat] for k in range(4)], axis=1)
            acc[...] += lax.dot_general(
                value.astype(BF16), block, (((1,), (1,)), ((), ())), preferred_element_type=F32
            )
            return carry

        lax.fori_loop(0, scores.shape[0] // 2, mix, 0)
        row_sum = jnp.sum(lane_sum[...], axis=1, keepdims=True)
        mixture = (acc[...] / row_sum).astype(BF16)
        for h in range(group_heads):
            value = jnp.dot(mixture[h * rows:(h + 1) * rows], va[group * group_heads + h], preferred_element_type=F32)
            att[z, group, :, h * vd:(h + 1) * vd] = value.astype(BF16)
        for way in (1, -1):
            att_forward(0, group, way)
        if group > 0:
            pass_on(1, group - 1)
        if group == 2:
            w_sends[3].wait_recv()
            w_sends[4].wait_recv()
            w_sends.append(w_copy(5, weight.at[far], weight.at[far], sibling, head))
            w_sends[5].start()

    def out_copy(to_z, column):
        return pltpu.make_async_remote_copy(
            src_ref=part.at[to_z, column],
            dst_ref=summed.at[head * 4 + mine],
            send_sem=out_send.at[to_z * 4 + column],
            recv_sem=out_recv.at[head * 4 + mine],
            device_id={"blk": z * 4 + column, "head": to_z},
            device_id_type=MESH,
        )

    def project(slots):
        lhs = [jnp.concatenate([att[slot, group] for group in range(GROUPS)], axis=1) for slot in slots]
        lhs = jnp.concatenate(lhs, axis=0) if len(slots) > 1 else lhs[0]

        def one(column, carry):
            value = jnp.dot(lhs, weight[column], preferred_element_type=F32).astype(BF16)
            for k, slot in enumerate(slots):
                part[slot, column] = value[k * rows:(k + 1) * rows]
                here = jnp.logical_and(slot == head, column == mine)

                @pl.when(here)
                def _():
                    summed[head * 4 + mine] = value[k * rows:(k + 1) * rows]

                @pl.when(jnp.logical_not(here))
                def _():
                    out_copy(slot, column).start()

            return carry

        lax.fori_loop(0, 4, one, 0)

    pass_on(1, GROUPS - 1)
    w_sends[2].wait_recv()
    w_sends[5].wait_recv()
    project([z])
    for step in (2, 3):
        for group in range(GROUPS):
            pass_on(step, group)
            if group == 1:
                project([wrap_z(z - step + 1), wrap_z(z + step - 1)])
    project([wrap_z(z - 3), wrap_z(z + 3)])
    for group in range(GROUPS):
        att_wait(wrap_z(z + 4), group)
    project([wrap_z(z + 4)])

    def arrive(i, carry):
        @pl.when(i != head * 4 + mine)
        def _():
            pltpu.make_async_remote_copy(
                src_ref=part.at[0, 0],
                dst_ref=summed.at[i],
                send_sem=out_send.at[0],
                recv_sem=out_recv.at[i],
                device_id={"blk": sibling, "head": head},
                device_id_type=MESH,
            ).wait_recv()

        return carry

    lax.fori_loop(0, 32, arrive, 0)
    for k in range(4):
        total = summed[k].astype(F32)
        for h in range(1, 8):
            total = total + summed[4 * h + k].astype(F32)
        out_ref[k * rows:(k + 1) * rows] = total.astype(BF16)

    for copy in key_sends + w_sends + list(att_sends.values()):
        copy.wait_send()

    def leave(i, carry):
        to_z, column = i // 4, i % 4

        @pl.when(jnp.logical_or(to_z != head, column != mine))
        def _():
            out_copy(to_z, column).wait_send()

        return carry

    lax.fori_loop(0, 32, leave, 0)


def body(query_nope, query_rope, key_absorb, value_absorb, out_weight, latent_cache, rope_key):
    rows = query_nope.shape[0]
    heads, nope, lat = key_absorb.shape
    rope, docs = rope_key.shape
    vd = value_absorb.shape[2]
    depth, columns = out_weight.shape
    pairs = heads * rows
    group_rows = pairs // GROUPS
    any_spec = pl.BlockSpec(memory_space=pl.ANY)
    dma = pltpu.SemaphoreType.DMA
    return pl.pallas_call(
        kernel,
        out_shape=jax.ShapeDtypeStruct((4 * rows, columns), BF16),
        in_specs=[any_spec] * 7,
        out_specs=pl.BlockSpec(memory_space=pltpu.VMEM),
        scratch_shapes=[
            pltpu.VMEM((32, lat + rope, docs), BF16),
            pltpu.VMEM((pairs, lat + rope), BF16),
            pltpu.VMEM(query_nope.shape, BF16),
            pltpu.VMEM(query_rope.shape, BF16),
            pltpu.VMEM(key_absorb.shape, BF16),
            pltpu.VMEM(value_absorb.shape, BF16),
            pltpu.VMEM((4, depth, columns), BF16),
            pltpu.VMEM((2, depth // 2, columns), BF16),
            pltpu.VMEM((16, pairs, 2 * docs), F32),
            pltpu.VMEM((pairs, docs), F32),
            pltpu.VMEM((group_rows, docs), F32),
            pltpu.VMEM((group_rows, lat), F32),
            pltpu.VMEM((Z, GROUPS, rows, heads // GROUPS * vd), BF16),
            pltpu.VMEM((Z, 4, rows, columns), BF16),
            pltpu.VMEM((32, rows, columns), BF16),
            dma((7,)),
            dma((31,)),
            dma((32,)),
            dma((6,)),
            dma((6,)),
            dma((28,)),
            dma((Z, GROUPS)),
            dma((32,)),
            dma((32,)),
        ],
        compiler_params=pltpu.CompilerParams(
            collective_id=0, has_side_effects=True, vmem_limit_bytes=60 * 1024 * 1024
        ),
    )(query_nope, query_rope, key_absorb, value_absorb, out_weight, latent_cache, rope_key)


def solution(mesh):
    in_specs = (
        P("blk", "head"),
        P("blk", "head"),
        P("head", None, None),
        P("head", None, None),
        P("head", "blk"),
        P(None, "blk"),
        P(None, "blk"),
    )
    return jax.shard_map(body, mesh=mesh, in_specs=in_specs, out_specs=P("head", "blk"), check_vma=False)
```

time: 286 us -> 87.1 us (0.30)
  the two profiles are of different devices: /device:TPU:32 before, /device:TPU:5 now
where the time goes in v1:
time: 87.1 us; the launch traced here: 87 us
  Pallas kernels  83.1 us (95%)
  local copies, waits for them, and re-layouts  3.91 us (4%)
    pallas_call x1, Pallas kernels, body(): pl.pallas_call(kernel, out_shape=jax.ShapeDtypeStruct((4 * rows, columns)...  83.1 us
    unnamed x1, local copies, waits for them, and re-layouts  2.25 us

profile of v1, /device:TPU:5, one launch (start us, length us, event | category | flops | bytes accessed | tf_op | source)
XLA Modules:
  0.0 87.0 jit_solution(16540630729883528208)
XLA Ops:
  0.0 2.3 %copy.8.w_hbm = bf16[2048,224]{1,0:T(8,128)(2,1)} copy(bf16[2048,224]{0,1:T(8,128)(2,1)} %param.11) | data formatting | bytes 1835008 | tf_op args[4]
  2.3 83.1 %shard_map.73 = bf16[256,224]{1,0:T(8,128)(2,1)} custom-call(bf16[64,2048]{1,0:T(8,128)(2,1)} %qn_hbm.1, bf16[64,1024]{1,0:T(8,128)(2,1)} %qr_hbm.1, bf16[16,128,512]{2,1,0:T(8,128)(2,1)} %ka_hbm.1, bf16[16,512,128]{2,1,0:T(8,128)(2,1)} %va_hbm.1, bf16[2048,224]{1,0:T(8,128)(2,1)} %copy.8.w_hbm, bf16[512,128]{1,0:T(8,128)(2,1)} %lat_hbm.1, ...), custom_call_target="tpu_custom_call" | custom-call | tf_op jit(solution)/shard_map/pallas_call | solution.py:402
  85.4 1.7 %copy.9 = bf16[256,224]{0,1:T(8,128)(2,1)} copy(bf16[256,224]{1,0:T(8,128)(2,1)} %shard_map.73) | data formatting | bytes 229376 | tf_op jit(solution)/shard_map/pallas_call | solution.py:402

commit v2 on v1

v2 whole, which is shorter than its diff:
```python
import functools
import math

import jax
import jax.numpy as jnp
from jax import lax
from jax.experimental import pallas as pl
from jax.experimental.pallas import tpu as pltpu
from jax.sharding import PartitionSpec as P

MESH = pl.DeviceIdType.MESH
F32 = jnp.float32
BF16 = jnp.bfloat16

Z = 8
X = 4
GROUPS = 4
PIECES = 4


def flip(value, bit):
    return value + bit - 2 * bit * (value // bit % 2)


def kernel(
    qn_hbm, qr_hbm, ka_hbm, va_hbm, w_hbm, lat_hbm, rk_hbm, out_ref,
    keys, keys_t, queries, qn, qr, ka, va, weight, scores, lane_max,
    att, part, summed,
    local_sem, key_send, key_recv, sib_send, sib_recv, w_send, w_recv, att_send, att_recv, out_send, out_recv,
):
    blk = lax.axis_index("blk")
    head = lax.axis_index("head")
    z = blk // 4
    mine = blk % 4
    yhi = mine // 2
    core = blk % 2
    x = head // 2
    sibling = flip(blk, 1)
    other_y = flip(blk, 2)
    head_y = flip(head, 1)
    side = 1 - 2 * core

    lat = lat_hbm.shape[0]
    rope = rk_hbm.shape[0]
    heads, nope = ka_hbm.shape[0], ka_hbm.shape[1]
    vd = va_hbm.shape[2]
    rows = qn_hbm.shape[0]
    group_heads = heads // GROUPS
    group_rows = group_heads * rows
    factor = (nope + rope) ** (-0.5) * math.log2(math.e)

    def wrap_z(value):
        return (value + 2 * Z) % Z

    def at_z(step):
        return wrap_z(z + step) * 4 + mine

    def at_x(step):
        return (x + step + X) % X * 2 + head % 2

    barrier = pltpu.get_barrier_semaphore()
    for step in (1, -1):
        pl.semaphore_signal(barrier, inc=1, device_id={"blk": at_z(step), "head": head}, device_id_type=MESH)

    def greet(i, carry):
        to_blk, to_head = z * 4 + i % 4, i // 4

        @pl.when(jnp.logical_or(to_blk != blk, to_head != head))
        def _():
            pl.semaphore_signal(barrier, inc=1, device_id={"blk": to_blk, "head": to_head}, device_id_type=MESH)

        return carry

    lax.fori_loop(0, 32, greet, 0)
    loads = [
        pltpu.make_async_copy(lat_hbm, keys.at[blk, pl.ds(0, lat)], local_sem.at[0]),
        pltpu.make_async_copy(rk_hbm, keys.at[blk, pl.ds(lat, rope)], local_sem.at[1]),
        pltpu.make_async_copy(qn_hbm, qn, local_sem.at[2]),
        pltpu.make_async_copy(qr_hbm, qr, local_sem.at[3]),
        pltpu.make_async_copy(ka_hbm, ka, local_sem.at[4]),
        pltpu.make_async_copy(w_hbm, weight.at[mine], local_sem.at[5]),
        pltpu.make_async_copy(va_hbm, va, local_sem.at[6]),
    ]
    for load in loads:
        load.start()

    pl.semaphore_wait(barrier, 33)

    depth = (lat + rope) // PIECES
    sends = []
    whole = []

    def piece_copy(index, slot, p, to_blk, to_head):
        at = keys.at[slot, pl.ds(pl.multiple_of(p * depth, 16), depth)]
        return pltpu.make_async_remote_copy(
            src_ref=at,
            dst_ref=at,
            send_sem=key_send.at[index, p],
            recv_sem=key_recv.at[slot, p],
            device_id={"blk": to_blk, "head": to_head},
            device_id_type=MESH,
        )

    def new_send():
        sends.append(None)
        return len(sends) - 1

    def piece_wait(slot, p):
        piece_copy(0, slot, p, sibling, head).wait_recv()

    def pieces_wait(slot):
        def one(p, carry):
            piece_wait(slot, p)
            return carry

        lax.fori_loop(0, PIECES, one, 0)

    def send_pieces(*targets):
        def one(p, carry):
            for index, slot, to_blk, to_head in targets:
                piece_copy(index, slot, p, to_blk, to_head).start()
            return carry

        lax.fori_loop(0, PIECES, one, 0)

    def sib_copy(index, slot):
        return pltpu.make_async_remote_copy(
            src_ref=keys.at[slot],
            dst_ref=keys.at[slot],
            send_sem=sib_send.at[index],
            recv_sem=sib_recv.at[slot],
            device_id={"blk": sibling, "head": head},
            device_id_type=MESH,
        )

    def to_sibling(slot):
        copy = sib_copy(len(whole), slot)
        copy.start()
        whole.append(copy)

    def w_copy(index, src, dst, to_blk):
        return pltpu.make_async_remote_copy(
            src_ref=src,
            dst_ref=dst,
            send_sem=w_send.at[index],
            recv_sem=w_recv.at[index],
            device_id={"blk": to_blk, "head": head},
            device_id_type=MESH,
        )

    carried = (yhi + x) % 2

    def carry_slot(step):
        return wrap_z(z + step) * 4 + carried * 2 + core

    def other_slot(step):
        return wrap_z(z + step) * 4 + (1 - carried) * 2 + core

    loads[0].wait()
    loads[1].wait()
    across, up, down = new_send(), new_send(), new_send()
    send_pieces((across, blk, other_y, head_y))

    @pl.when(x % 2 == 0)
    def _():
        send_pieces((up, blk, at_z(1), head), (down, blk, at_z(-1), head))

    to_sibling(blk)

    lane_max[...] = jnp.full_like(lane_max, -jnp.inf)

    for index in (2, 3, 4):
        loads[index].wait()
    for h in range(heads):
        product = jnp.dot(qn[:, h * nope:(h + 1) * nope], ka[h], preferred_element_type=F32)
        queries[h * rows:(h + 1) * rows, 0:lat] = product.astype(BF16)
        queries[h * rows:(h + 1) * rows, lat:lat + rope] = qr[:, h * rope:(h + 1) * rope]

    def across_piece(p, carry):
        piece_wait(flip(blk, 2), p)

        @pl.when(x % 2 == 1)
        def _():
            piece_copy(up, flip(blk, 2), p, at_z(1), head).start()
            piece_copy(down, flip(blk, 2), p, at_z(-1), head).start()

        return carry

    lax.fori_loop(0, PIECES, across_piece, 0)
    to_sibling(flip(blk, 2))

    own_w = weight.at[mine]
    far = flip(mine, 2)
    loads[5].wait()
    w_sends = [w_copy(0, own_w, own_w, other_y), w_copy(1, own_w, own_w, sibling)]
    for copy in w_sends:
        copy.start()

    def unit(step, half_y):
        base = wrap_z(z + step) * 4 + half_y * 2
        sib_copy(0, base + 1 - core).wait_recv()
        block = jnp.concatenate([keys[base], keys[base + 1]], axis=1)
        product = jnp.dot(queries[...], block, preferred_element_type=F32)
        scores[base // 2] = product
        keys_t[base // 2] = block[0:lat].T
        width = block.shape[1] // 2
        lane_max[...] = jnp.maximum(lane_max[...], jnp.maximum(product[:, :width], product[:, width:]))

    def units(i, carry_step, other_step):
        late = i // 2
        step = (1 - 2 * (i % 2)) * (carry_step + (other_step - carry_step) * late)
        unit(step, (carried + late) % 2)

    def advance(step):
        ways = (1, -1)
        forward = [new_send() for _ in ways] if step < 3 else [new_send()]
        along_x = [new_send() for _ in ways]

        def one(p, carry):
            for k, way in enumerate(ways):
                slot = carry_slot(-way * step)
                piece_wait(slot, p)
                if step < 3:
                    piece_copy(forward[k], slot, p, at_z(way), head).start()
            if step == 3:
                piece_copy(forward[0], carry_slot(-side * 3), p, at_z(side), head).start()
            for k, way in enumerate(ways):
                piece_copy(along_x[k], carry_slot(-way * step), p, blk, at_x(way)).start()
            if step == 3:
                units(p, 2, 1)
            else:
                @pl.when(p % 2 == 1)
                def _():
                    if step == 1:
                        unit(0, (yhi + p // 2) % 2)
                    else:
                        unit(1 - 2 * (p // 2), carried)

            return carry

        lax.fori_loop(0, PIECES, one, 0)
        for way in ways:
            to_sibling(carry_slot(-way * step))
        if step > 1:
            for way in ways:
                pieces_wait(other_slot(-way * (step - 1)))
                to_sibling(other_slot(-way * (step - 1)))

    for step in (1, 2, 3):
        advance(step)
    last = new_send()

    def last_piece(p, carry):
        piece_wait(carry_slot(4), p)
        piece_copy(last, carry_slot(4), p, blk, at_x(side)).start()
        units(p, 3, 2)
        return carry

    lax.fori_loop(0, PIECES, last_piece, 0)
    to_sibling(carry_slot(4))
    for way in (1, -1):
        pieces_wait(other_slot(-way * 3))
        to_sibling(other_slot(-way * 3))
    pieces_wait(other_slot(4))
    to_sibling(other_slot(4))

    def tail_units(i, carry):
        middle = (i + 1) // 2 % 2
        step = 4 * (1 - middle) + middle * 3 * (3 - 2 * i)
        unit(step, (carried + (i + 2) // 3) % 2)
        return carry

    lax.fori_loop(0, 4, tail_units, 0)

    att_sends = {}

    def att_copy(index, slot, group, to_blk):
        return pltpu.make_async_remote_copy(
            src_ref=att.at[slot, group],
            dst_ref=att.at[slot, group],
            send_sem=att_send.at[index],
            recv_sem=att_recv.at[slot, group],
            device_id={"blk": to_blk, "head": head},
            device_id_type=MESH,
        )

    def att_forward(step, group, way):
        copy = att_copy(len(att_sends), wrap_z(z - way * step), group, at_z(way))
        copy.start()
        att_sends[step, group, way] = copy

    def att_wait(slot, group):
        att_copy(0, slot, group, at_z(1)).wait_recv()

    def pass_on(step, group):
        for way in (1, -1):
            att_wait(wrap_z(z - way * step), group)
            if step < 3 or (group % 2 == 0) == (way == 1):
                att_forward(step, group, way)

    loads[6].wait()
    for group in range(GROUPS):
        rows_at = pl.ds(group * group_rows, group_rows)
        top = jnp.max(lane_max[rows_at], axis=1, keepdims=True)
        count = scores.shape[0]
        weights, total = [], None
        for u in range(count):
            value = jnp.exp2((scores[u, rows_at] - top) * factor)
            weights.append(value.astype(BF16))
            width = value.shape[1] // 2
            value = value[:, :width] + value[:, width:]
            total = value if total is None else total + value
        mixed = jnp.dot(
            jnp.concatenate(weights, axis=1), keys_t[...].reshape(-1, lat), preferred_element_type=F32
        )
        mixture = (mixed / jnp.sum(total, axis=1, keepdims=True)).astype(BF16)
        for h in range(group_heads):
            value = jnp.dot(mixture[h * rows:(h + 1) * rows], va[group * group_heads + h], preferred_element_type=F32)
            att[z, group, :, h * vd:(h + 1) * vd] = value.astype(BF16)
        for way in (1, -1):
            att_forward(0, group, way)
        if group == 2:
            w_sends[0].wait_recv()
            w_sends.append(w_copy(2, weight.at[far], weight.at[far], sibling))
            w_sends[2].start()

    def out_copy(to_z, column):
        return pltpu.make_async_remote_copy(
            src_ref=part.at[to_z, column],
            dst_ref=summed.at[head * 4 + mine],
            send_sem=out_send.at[to_z * 4 + column],
            recv_sem=out_recv.at[head * 4 + mine],
            device_id={"blk": z * 4 + column, "head": to_z},
            device_id_type=MESH,
        )

    def project(slots):
        lhs = [jnp.concatenate([att[slot, group] for group in range(GROUPS)], axis=1) for slot in slots]
        lhs = jnp.concatenate(lhs, axis=0) if len(slots) > 1 else lhs[0]

        def one(column, carry):
            value = lax.dot_general(
                lhs, weight[column], (((1,), (1,)), ((), ())), preferred_element_type=F32
            ).astype(BF16)
            for k, slot in enumerate(slots):
                part[slot, column] = value[k * rows:(k + 1) * rows]
                here = jnp.logical_and(slot == head, column == mine)

                @pl.when(here)
                def _():
                    summed[head * 4 + mine] = value[k * rows:(k + 1) * rows]

                @pl.when(jnp.logical_not(here))
                def _():
                    out_copy(slot, column).start()

            return carry

        lax.fori_loop(0, 4, one, 0)

    for group in range(GROUPS):
        pass_on(1, group)
    w_sends[1].wait_recv()
    w_sends[2].wait_recv()
    project([z])
    for step in (2, 3):
        for group in range(GROUPS):
            pass_on(step, group)
            if group == 1:
                project([wrap_z(z - step + 1), wrap_z(z + step - 1)])
    project([wrap_z(z - 3), wrap_z(z + 3)])
    for group in range(GROUPS):
        att_wait(wrap_z(z + 4), group)
    project([wrap_z(z + 4)])

    def arrive(i, carry):
        @pl.when(i != head * 4 + mine)
        def _():
            pltpu.make_async_remote_copy(
                src_ref=part.at[0, 0],
                dst_ref=summed.at[i],
                send_sem=out_send.at[0],
                recv_sem=out_recv.at[i],
                device_id={"blk": sibling, "head": head},
                device_id_type=MESH,
            ).wait_recv()

        return carry

    lax.fori_loop(0, 32, arrive, 0)
    totals = []
    for k in range(4):
        total = summed[k].astype(F32)
        for h in range(1, 8):
            total = total + summed[4 * h + k].astype(F32)
        totals.append(total)

    out_ref[...] = jnp.concatenate(totals, axis=0).T.astype(BF16)

    def left(i, carry):
        piece_copy(i // PIECES, blk, i % PIECES, sibling, head).wait_send()
        return carry

    lax.fori_loop(0, len(sends) * PIECES, left, 0)
    for copy in whole + w_sends + list(att_sends.values()):
        copy.wait_send()

    def leave(i, carry):
        to_z, column = i // 4, i % 4

        @pl.when(jnp.logical_or(to_z != head, column != mine))
        def _():
            out_copy(to_z, column).wait_send()

        return carry

    lax.fori_loop(0, 32, leave, 0)


def body(query_nope, query_rope, key_absorb, value_absorb, out_weight, latent_cache, rope_key):
    out_weight = out_weight.T
    rows = query_nope.shape[0]
    heads, nope, lat = key_absorb.shape
    rope, docs = rope_key.shape
    vd = value_absorb.shape[2]
    columns, depth = out_weight.shape
    pairs = heads * rows
    any_spec = pl.BlockSpec(memory_space=pl.ANY)
    dma = pltpu.SemaphoreType.DMA
    return pl.pallas_call(
        kernel,
        out_shape=jax.ShapeDtypeStruct((columns, 4 * rows), BF16),
        in_specs=[any_spec] * 7,
        out_specs=pl.BlockSpec(memory_space=pltpu.VMEM),
        scratch_shapes=[
            pltpu.VMEM((32, lat + rope, docs), BF16),
            pltpu.VMEM((16, 2 * docs, lat), BF16),
            pltpu.VMEM((pairs, lat + rope), BF16),
            pltpu.VMEM(query_nope.shape, BF16),
            pltpu.VMEM(query_rope.shape, BF16),
            pltpu.VMEM(key_absorb.shape, BF16),
            pltpu.VMEM(value_absorb.shape, BF16),
            pltpu.VMEM((4, columns, depth), BF16),
            pltpu.VMEM((16, pairs, 2 * docs), F32),
            pltpu.VMEM((pairs, docs), F32),
            pltpu.VMEM((Z, GROUPS, rows, heads // GROUPS * vd), BF16),
            pltpu.VMEM((Z, 4, rows, columns), BF16),
            pltpu.VMEM((32, rows, columns), BF16),
            dma((7,)),
            dma((15, PIECES)),
            dma((32, PIECES)),
            dma((16,)),
            dma((32,)),
            dma((3,)),
            dma((3,)),
            dma((28,)),
            dma((Z, GROUPS)),
            dma((32,)),
            dma((32,)),
        ],
        compiler_params=pltpu.CompilerParams(
            collective_id=0, has_side_effects=True, vmem_limit_bytes=60 * 1024 * 1024
        ),
    )(query_nope, query_rope, key_absorb, value_absorb, out_weight, latent_cache, rope_key).T


def solution(mesh):
    in_specs = (
        P("blk", "head"),
        P("blk", "head"),
        P("head", None, None),
        P("head", None, None),
        P("head", "blk"),
        P(None, "blk"),
        P(None, "blk"),
    )
    return jax.shard_map(body, mesh=mesh, in_specs=in_specs, out_specs=P("head", "blk"), check_vma=False)
```

time: 87.1 us -> 81.3 us (0.933)
  Pallas kernels: 83.1 us -> 79.6 us
  local copies, waits for them, and re-layouts: 3.91 us -> 1.55 us
    pallas_call x1, Pallas kernels: 83.1 us -> 79.6 us  [body(): pl.pallas_call(kernel, out_shape=jax.ShapeDtypeStruct((columns, 4 * rows)...]
    pallas_call x1 -> x0, local copies, waits for them, and re-layouts: 1.65 us -> none  [body(): pl.pallas_call(kernel, out_shape=jax.ShapeDtypeStruct((4 * rows, columns)...]
where the time goes in v2:
time: 81.3 us; the launch traced here: 81.2 us
  Pallas kernels  79.6 us (98%)
  local copies, waits for them, and re-layouts  1.55 us (2%)
    pallas_call x1, Pallas kernels, body(): pl.pallas_call(kernel, out_shape=jax.ShapeDtypeStruct((columns, 4 * rows)...  79.6 us

profile of v2, /device:TPU:5, one launch (start us, length us, event | category | flops | bytes accessed | tf_op | source)
XLA Modules:
  0.0 81.2 jit_solution(17029297848532979010)
XLA Ops:
  0.0 79.6 %shard_map.73 = bf16[224,256]{1,0:T(8,128)(2,1)} custom-call(bf16[64,2048]{1,0:T(8,128)(2,1)} %qn_hbm.1, bf16[64,1024]{1,0:T(8,128)(2,1)} %qr_hbm.1, bf16[16,128,512]{2,1,0:T(8,128)(2,1)} %ka_hbm.1, bf16[16,512,128]{2,1,0:T(8,128)(2,1)} %va_hbm.1, bf16[224,2048]{1,0:T(8,128)(2,1)} %bitcast.2, bf16[512,128]{1,0:T(8,128)(2,1)} %lat_hbm.1, bf16[64,128]{1,0:T(8,128)(2,1)} %rk_hbm.1), custom_call_target="tpu_custom_call" | custom-call | tf_op jit(solution)/shard_map/pallas_call | solution.py:430
  79.6 1.6 %copy.9 = bf16[256,224]{0,1:T(8,128)(2,1)} copy(bf16[256,224]{0,1:T(8,128)(2,1)} %bitcast.3) | data formatting | bytes 229376

commit v3 on v2

--- a/solution.py
+++ b/solution.py
@@ -62,16 +62,9 @@
     for step in (1, -1):
         pl.semaphore_signal(barrier, inc=1, device_id={"blk": at_z(step), "head": head}, device_id_type=MESH)
 
-    def greet(i, carry):
-        to_blk, to_head = z * 4 + i % 4, i // 4
-
-        @pl.when(jnp.logical_or(to_blk != blk, to_head != head))
-        def _():
-            pl.semaphore_signal(barrier, inc=1, device_id={"blk": to_blk, "head": to_head}, device_id_type=MESH)
-
-        return carry
-
-    lax.fori_loop(0, 32, greet, 0)
+    for to_blk, to_head in ((blk, at_x(1)), (blk, at_x(-1)), (other_y, head_y), (other_y, head), (sibling, head)):
+        pl.semaphore_signal(barrier, inc=1, device_id={"blk": to_blk, "head": to_head}, device_id_type=MESH)
+
     loads = [
         pltpu.make_async_copy(lat_hbm, keys.at[blk, pl.ds(0, lat)], local_sem.at[0]),
         pltpu.make_async_copy(rk_hbm, keys.at[blk, pl.ds(lat, rope)], local_sem.at[1]),
@@ -84,7 +77,7 @@
     for load in loads:
         load.start()
 
-    pl.semaphore_wait(barrier, 33)
+    pl.semaphore_wait(barrier, 7)
 
     depth = (lat + rope) // PIECES
     sends = []
@@ -358,17 +351,17 @@
 
         lax.fori_loop(0, 4, one, 0)
 
-    for group in range(GROUPS):
-        pass_on(1, group)
+    pass_on(1, 0)
     w_sends[1].wait_recv()
     w_sends[2].wait_recv()
     project([z])
+    for group in range(1, GROUPS):
+        pass_on(1, group)
+    project([wrap_z(z - 1), wrap_z(z + 1)])
     for step in (2, 3):
         for group in range(GROUPS):
             pass_on(step, group)
-            if group == 1:
-                project([wrap_z(z - step + 1), wrap_z(z + step - 1)])
-    project([wrap_z(z - 3), wrap_z(z + 3)])
+        project([wrap_z(z - step), wrap_z(z + step)])
     for group in range(GROUPS):
         att_wait(wrap_z(z + 4), group)
     project([wrap_z(z + 4)])

time: 81.3 us -> 80 us (0.984)
  Pallas kernels: 79.6 us -> 78.3 us
    pallas_call x1, Pallas kernels: 79.6 us -> 78.3 us  [body(): pl.pallas_call(kernel, out_shape=jax.ShapeDtypeStruct((columns, 4 * rows)...]
where the time goes in v3:
time: 80 us; the launch traced here: 79.9 us
  Pallas kernels  78.3 us (98%)
  local copies, waits for them, and re-layouts  1.55 us (2%)
    pallas_call x1, Pallas kernels, body(): pl.pallas_call(kernel, out_shape=jax.ShapeDtypeStruct((columns, 4 * rows)...  78.3 us

profile of v3, /device:TPU:5, one launch (start us, length us, event | category | flops | bytes accessed | tf_op | source)
XLA Modules:
  0.0 79.9 jit_solution(8113002085451626020)
XLA Ops:
  0.0 78.3 %shard_map.73 = bf16[224,256]{1,0:T(8,128)(2,1)} custom-call(bf16[64,2048]{1,0:T(8,128)(2,1)} %qn_hbm.1, bf16[64,1024]{1,0:T(8,128)(2,1)} %qr_hbm.1, bf16[16,128,512]{2,1,0:T(8,128)(2,1)} %ka_hbm.1, bf16[16,512,128]{2,1,0:T(8,128)(2,1)} %va_hbm.1, bf16[224,2048]{1,0:T(8,128)(2,1)} %bitcast.2, bf16[512,128]{1,0:T(8,128)(2,1)} %lat_hbm.1, bf16[64,128]{1,0:T(8,128)(2,1)} %rk_hbm.1), custom_call_target="tpu_custom_call" | custom-call | tf_op jit(solution)/shard_map/pallas_call | solution.py:423
  78.3 1.6 %copy.9 = bf16[256,224]{0,1:T(8,128)(2,1)} copy(bf16[256,224]{0,1:T(8,128)(2,1)} %bitcast.3) | data formatting | bytes 229376

commit v4 on v3

--- a/solution.py
+++ b/solution.py
@@ -24,8 +24,8 @@
 
 def kernel(
     qn_hbm, qr_hbm, ka_hbm, va_hbm, w_hbm, lat_hbm, rk_hbm, out_ref,
-    keys, keys_t, queries, qn, qr, ka, va, weight, scores, lane_max,
-    att, part, summed,
+    keys, keys_t, queries, qn, qr, ka, va, weight, scores, lane_max, top, lane_sum, acc,
+    att, part, summed, totals,
     local_sem, key_send, key_recv, sib_send, sib_recv, w_send, w_recv, att_send, att_recv, out_send, out_recv,
 ):
     blk = lax.axis_index("blk")
@@ -161,6 +161,9 @@
     to_sibling(blk)
 
     lane_max[...] = jnp.full_like(lane_max, -jnp.inf)
+    top[...] = jnp.full_like(top, -jnp.inf)
+    lane_sum[...] = jnp.zeros_like(lane_sum)
+    acc[...] = jnp.zeros_like(acc)
 
     for index in (2, 3, 4):
         loads[index].wait()
@@ -189,20 +192,36 @@
     for copy in w_sends:
         copy.start()
 
-    def unit(step, half_y):
-        base = wrap_z(z + step) * 4 + half_y * 2
-        sib_copy(0, base + 1 - core).wait_recv()
-        block = jnp.concatenate([keys[base], keys[base + 1]], axis=1)
+    def units(*places):
+        bases = [wrap_z(z + step) * 4 + half_y * 2 for step, half_y in places]
+        for base in bases:
+            sib_copy(0, base + 1 - core).wait_recv()
+        block = jnp.concatenate([keys[base + k] for base in bases for k in range(2)], axis=1)
         product = jnp.dot(queries[...], block, preferred_element_type=F32)
-        scores[base // 2] = product
-        keys_t[base // 2] = block[0:lat].T
-        width = block.shape[1] // 2
-        lane_max[...] = jnp.maximum(lane_max[...], jnp.maximum(product[:, :width], product[:, width:]))
-
-    def units(i, carry_step, other_step):
-        late = i // 2
-        step = (1 - 2 * (i % 2)) * (carry_step + (other_step - carry_step) * late)
-        unit(step, (carried + late) % 2)
+        first, others = product[0:group_rows], product[group_rows:]
+        turned = block[0:lat].T
+        width = block.shape[1] // 4
+        for k, base in enumerate(bases):
+            scores[base // 2] = others[:, 2 * k * width:2 * (k + 1) * width]
+            keys_t[base // 2] = turned[2 * k * width:2 * (k + 1) * width]
+        largest = jnp.maximum(
+            jnp.maximum(others[:, :width], others[:, width:2 * width]),
+            jnp.maximum(others[:, 2 * width:3 * width], others[:, 3 * width:]),
+        )
+        lane_max[...] = jnp.maximum(lane_max[...], largest)
+        before = top[...]
+        now = jnp.maximum(before, jnp.max(first, axis=1, keepdims=True))
+        shrink = jnp.exp2((before - now) * factor)
+        value = jnp.exp2((first - jnp.concatenate([now] * 4, axis=1)) * factor)
+        top[...] = now
+        lane_sum[...] = lane_sum[...] * shrink + (
+            (value[:, :width] + value[:, width:2 * width]) + (value[:, 2 * width:3 * width] + value[:, 3 * width:])
+        )
+        grown = jnp.dot(value.astype(BF16), turned, preferred_element_type=F32)
+        acc[...] = acc[...] * jnp.concatenate([shrink] * (lat // width), axis=1) + grown
+
+    def both(step, half_y):
+        units((step, half_y), (-step, half_y))
 
     def advance(step):
         ways = (1, -1)
@@ -219,51 +238,42 @@
                 piece_copy(forward[0], carry_slot(-side * 3), p, at_z(side), head).start()
             for k, way in enumerate(ways):
                 piece_copy(along_x[k], carry_slot(-way * step), p, blk, at_x(way)).start()
-            if step == 3:
-                units(p, 2, 1)
-            else:
-                @pl.when(p % 2 == 1)
-                def _():
-                    if step == 1:
-                        unit(0, (yhi + p // 2) % 2)
-                    else:
-                        unit(1 - 2 * (p // 2), carried)
-
             return carry
 
         lax.fori_loop(0, PIECES, one, 0)
         for way in ways:
             to_sibling(carry_slot(-way * step))
-        if step > 1:
-            for way in ways:
-                pieces_wait(other_slot(-way * (step - 1)))
-                to_sibling(other_slot(-way * (step - 1)))
-
-    for step in (1, 2, 3):
-        advance(step)
+
+    def others(step):
+        for way in (1, -1):
+            pieces_wait(other_slot(-way * step))
+            to_sibling(other_slot(-way * step))
+
+    advance(1)
+    units((0, yhi), (0, 1 - yhi))
+    advance(2)
+    both(1, carried)
+    advance(3)
+    others(1)
+    both(2, carried)
     last = new_send()
 
     def last_piece(p, carry):
         piece_wait(carry_slot(4), p)
         piece_copy(last, carry_slot(4), p, blk, at_x(side)).start()
-        units(p, 3, 2)
         return carry
 
     lax.fori_loop(0, PIECES, last_piece, 0)
     to_sibling(carry_slot(4))
-    for way in (1, -1):
-        pieces_wait(other_slot(-way * 3))
-        to_sibling(other_slot(-way * 3))
+    others(2)
+    both(1, 1 - carried)
+    both(3, carried)
+    others(3)
+    both(2, 1 - carried)
     pieces_wait(other_slot(4))
     to_sibling(other_slot(4))
-
-    def tail_units(i, carry):
-        middle = (i + 1) // 2 % 2
-        step = 4 * (1 - middle) + middle * 3 * (3 - 2 * i)
-        unit(step, (carried + (i + 2) // 3) % 2)
-        return carry
-
-    lax.fori_loop(0, 4, tail_units, 0)
+    both(3, 1 - carried)
+    units((4, carried), (4, 1 - carried))
 
     att_sends = {}
 
@@ -292,13 +302,12 @@
                 att_forward(step, group, way)
 
     loads[6].wait()
-    for group in range(GROUPS):
-        rows_at = pl.ds(group * group_rows, group_rows)
-        top = jnp.max(lane_max[rows_at], axis=1, keepdims=True)
-        count = scores.shape[0]
+    def mix(start):
+        rows_at = pl.ds(start, group_rows)
+        largest = jnp.max(lane_max[rows_at], axis=1, keepdims=True)
         weights, total = [], None
-        for u in range(count):
-            value = jnp.exp2((scores[u, rows_at] - top) * factor)
+        for u in range(scores.shape[0]):
+            value = jnp.exp2((scores[u, rows_at] - largest) * factor)
             weights.append(value.astype(BF16))
             width = value.shape[1] // 2
             value = value[:, :width] + value[:, width:]
@@ -306,6 +315,13 @@
         mixed = jnp.dot(
             jnp.concatenate(weights, axis=1), keys_t[...].reshape(-1, lat), preferred_element_type=F32
         )
+        return mixed, total
+
+    for group in range(GROUPS):
+        if group == 0:
+            mixed, total = acc[...], lane_sum[...]
+        else:
+            mixed, total = mix((group - 1) * group_rows)
         mixture = (mixed / jnp.sum(total, axis=1, keepdims=True)).astype(BF16)
         for h in range(group_heads):
             value = jnp.dot(mixture[h * rows:(h + 1) * rows], va[group * group_heads + h], preferred_element_type=F32)
@@ -327,6 +343,18 @@
             device_id_type=MESH,
         )
 
+    columns = out_ref.shape[0]
+    rest = columns - 128
+    strip = rows // 4
+    spare = 128 - rest
+
+    def pack(ref, value):
+        ref[0:rows] = value[:, 0:128]
+        for i in range(3):
+            at = rows + i * strip
+            ref[at:at + strip, 0:rest] = value[i * strip:(i + 1) * strip, 128:columns]
+            ref[at:at + strip, rest:128] = value[3 * strip:rows, 128 + i * spare:128 + (i + 1) * spare]
+
     def project(slots):
         lhs = [jnp.concatenate([att[slot, group] for group in range(GROUPS)], axis=1) for slot in slots]
         lhs = jnp.concatenate(lhs, axis=0) if len(slots) > 1 else lhs[0]
@@ -336,12 +364,12 @@
                 lhs, weight[column], (((1,), (1,)), ((), ())), preferred_element_type=F32
             ).astype(BF16)
             for k, slot in enumerate(slots):
-                part[slot, column] = value[k * rows:(k + 1) * rows]
+                pack(part.at[slot, column], value[k * rows:(k + 1) * rows])
                 here = jnp.logical_and(slot == head, column == mine)
 
                 @pl.when(here)
                 def _():
-                    summed[head * 4 + mine] = value[k * rows:(k + 1) * rows]
+                    summed[head * 4 + mine] = part[slot, column]
 
                 @pl.when(jnp.logical_not(here))
                 def _():
@@ -381,14 +409,17 @@
         return carry
 
     lax.fori_loop(0, 32, arrive, 0)
-    totals = []
     for k in range(4):
         total = summed[k].astype(F32)
         for h in range(1, 8):
             total = total + summed[4 * h + k].astype(F32)
-        totals.append(total)
-
-    out_ref[...] = jnp.concatenate(totals, axis=0).T.astype(BF16)
+        at = k * rows
+        totals[at:at + rows, 0:128] = total[0:rows]
+        for i in range(3):
+            piece = total[rows + i * strip:rows + (i + 1) * strip]
+            totals[at + i * strip:at + (i + 1) * strip, 128:columns] = piece[:, 0:rest]
+            totals[at + 3 * strip:at + rows, 128 + i * spare:128 + (i + 1) * spare] = piece[:, rest:128]
+    out_ref[...] = totals[...].T.astype(BF16)
 
     def left(i, carry):
         piece_copy(i // PIECES, blk, i % PIECES, sibling, head).wait_send()
@@ -418,6 +449,7 @@
     vd = value_absorb.shape[2]
     columns, depth = out_weight.shape
     pairs = heads * rows
+    group_rows = pairs // GROUPS
     any_spec = pl.BlockSpec(memory_space=pl.ANY)
     dma = pltpu.SemaphoreType.DMA
     return pl.pallas_call(
@@ -434,11 +466,15 @@
             pltpu.VMEM(key_absorb.shape, BF16),
             pltpu.VMEM(value_absorb.shape, BF16),
             pltpu.VMEM((4, columns, depth), BF16),
-            pltpu.VMEM((16, pairs, 2 * docs), F32),
-            pltpu.VMEM((pairs, docs), F32),
+            pltpu.VMEM((16, pairs - group_rows, 2 * docs), F32),
+            pltpu.VMEM((pairs - group_rows, docs), F32),
+            pltpu.VMEM((group_rows, docs), F32),
+            pltpu.VMEM((group_rows, docs), F32),
+            pltpu.VMEM((group_rows, lat), F32),
             pltpu.VMEM((Z, GROUPS, rows, heads // GROUPS * vd), BF16),
-            pltpu.VMEM((Z, 4, rows, columns), BF16),
-            pltpu.VMEM((32, rows, columns), BF16),
+            pltpu.VMEM((Z, 4, rows * columns // 128, 128), BF16),
+            pltpu.VMEM((32, rows * columns // 128, 128), BF16),
+            pltpu.VMEM((4 * rows, columns), F32),
             dma((7,)),
             dma((15, PIECES)),
             dma((32, PIECES)),

time: 80 us -> 77.1 us (0.964)
  Pallas kernels: 78.3 us -> 75.5 us
    pallas_call x1, Pallas kernels: 78.3 us -> 75.5 us  [body(): pl.pallas_call(kernel, out_shape=jax.ShapeDtypeStruct((columns, 4 * rows)...]
where the time goes in v4:
time: 77.1 us; the launch traced here: 77 us
  Pallas kernels  75.5 us (98%)
  local copies, waits for them, and re-layouts  1.55 us (2%)
    pallas_call x1, Pallas kernels, body(): pl.pallas_call(kernel, out_shape=jax.ShapeDtypeStruct((columns, 4 * rows)...  75.5 us
    unnamed x1, local copies, waits for them, and re-layouts  1.55 us

profile of v4, /device:TPU:5, one launch (start us, length us, event | category | flops | bytes accessed | tf_op | source)
XLA Modules:
  0.0 77.0 jit_solution(13544351141358250708)
XLA Ops:
  0.0 75.5 %shard_map.73 = bf16[224,256]{1,0:T(8,128)(2,1)} custom-call(bf16[64,2048]{1,0:T(8,128)(2,1)} %qn_hbm.1, bf16[64,1024]{1,0:T(8,128)(2,1)} %qr_hbm.1, bf16[16,128,512]{2,1,0:T(8,128)(2,1)} %ka_hbm.1, bf16[16,512,128]{2,1,0:T(8,128)(2,1)} %va_hbm.1, bf16[224,2048]{1,0:T(8,128)(2,1)} %bitcast.2, bf16[512,128]{1,0:T(8,128)(2,1)} %lat_hbm.1, bf16[64,128]{1,0:T(8,128)(2,1)} %rk_hbm.1), custom_call_target="tpu_custom_call" | custom-call | tf_op jit(solution)/shard_map/pallas_call | solution.py:455
  75.5 1.6 %copy.9 = bf16[256,224]{0,1:T(8,128)(2,1)} copy(bf16[256,224]{0,1:T(8,128)(2,1)} %bitcast.3) | data formatting | bytes 229376

commit v5 on v4

--- a/solution.py
+++ b/solution.py
@@ -24,7 +24,7 @@
 
 def kernel(
     qn_hbm, qr_hbm, ka_hbm, va_hbm, w_hbm, lat_hbm, rk_hbm, out_ref,
-    keys, keys_t, queries, qn, qr, ka, va, weight, scores, lane_max, top, lane_sum, acc,
+    keys, queries, qn, qr, ka, va, weight, top, lane_sum, acc,
     att, part, summed, totals,
     local_sem, key_send, key_recv, sib_send, sib_recv, w_send, w_recv, att_send, att_recv, out_send, out_recv,
 ):
@@ -160,7 +160,6 @@
 
     to_sibling(blk)
 
-    lane_max[...] = jnp.full_like(lane_max, -jnp.inf)
     top[...] = jnp.full_like(top, -jnp.inf)
     lane_sum[...] = jnp.zeros_like(lane_sum)
     acc[...] = jnp.zeros_like(acc)
@@ -197,18 +196,9 @@
         for base in bases:
             sib_copy(0, base + 1 - core).wait_recv()
         block = jnp.concatenate([keys[base + k] for base in bases for k in range(2)], axis=1)
-        product = jnp.dot(queries[...], block, preferred_element_type=F32)
-        first, others = product[0:group_rows], product[group_rows:]
+        first = jnp.dot(queries[...], block, preferred_element_type=F32)
         turned = block[0:lat].T
         width = block.shape[1] // 4
-        for k, base in enumerate(bases):
-            scores[base // 2] = others[:, 2 * k * width:2 * (k + 1) * width]
-            keys_t[base // 2] = turned[2 * k * width:2 * (k + 1) * width]
-        largest = jnp.maximum(
-            jnp.maximum(others[:, :width], others[:, width:2 * width]),
-            jnp.maximum(others[:, 2 * width:3 * width], others[:, 3 * width:]),
-        )
-        lane_max[...] = jnp.maximum(lane_max[...], largest)
         before = top[...]
         now = jnp.maximum(before, jnp.max(first, axis=1, keepdims=True))
         shrink = jnp.exp2((before - now) * factor)
@@ -302,26 +292,9 @@
                 att_forward(step, group, way)
 
     loads[6].wait()
-    def mix(start):
-        rows_at = pl.ds(start, group_rows)
-        largest = jnp.max(lane_max[rows_at], axis=1, keepdims=True)
-        weights, total = [], None
-        for u in range(scores.shape[0]):
-            value = jnp.exp2((scores[u, rows_at] - largest) * factor)
-            weights.append(value.astype(BF16))
-            width = value.shape[1] // 2
-            value = value[:, :width] + value[:, width:]
-            total = value if total is None else total + value
-        mixed = jnp.dot(
-            jnp.concatenate(weights, axis=1), keys_t[...].reshape(-1, lat), preferred_element_type=F32
-        )
-        return mixed, total
-
     for group in range(GROUPS):
-        if group == 0:
-            mixed, total = acc[...], lane_sum[...]
-        else:
-            mixed, total = mix((group - 1) * group_rows)
+        rows_at = pl.ds(group * group_rows, group_rows)
+        mixed, total = acc[rows_at], lane_sum[rows_at]
         mixture = (mixed / jnp.sum(total, axis=1, keepdims=True)).astype(BF16)
         for h in range(group_heads):
             value = jnp.dot(mixture[h * rows:(h + 1) * rows], va[group * group_heads + h], preferred_element_type=F32)
@@ -449,7 +422,6 @@
     vd = value_absorb.shape[2]
     columns, depth = out_weight.shape
     pairs = heads * rows
-    group_rows = pairs // GROUPS
     any_spec = pl.BlockSpec(memory_space=pl.ANY)
     dma = pltpu.SemaphoreType.DMA
     return pl.pallas_call(
@@ -459,18 +431,15 @@
         out_specs=pl.BlockSpec(memory_space=pltpu.VMEM),
         scratch_shapes=[
             pltpu.VMEM((32, lat + rope, docs), BF16),
-            pltpu.VMEM((16, 2 * docs, lat), BF16),
             pltpu.VMEM((pairs, lat + rope), BF16),
             pltpu.VMEM(query_nope.shape, BF16),
             pltpu.VMEM(query_rope.shape, BF16),
             pltpu.VMEM(key_absorb.shape, BF16),
             pltpu.VMEM(value_absorb.shape, BF16),
             pltpu.VMEM((4, columns, depth), BF16),
-            pltpu.VMEM((16, pairs - group_rows, 2 * docs), F32),
-            pltpu.VMEM((pairs - group_rows, docs), F32),
-            pltpu.VMEM((group_rows, docs), F32),
-            pltpu.VMEM((group_rows, docs), F32),
-            pltpu.VMEM((group_rows, lat), F32),
+            pltpu.VMEM((pairs, docs), F32),
+            pltpu.VMEM((pairs, docs), F32),
+            pltpu.VMEM((pairs, lat), F32),
             pltpu.VMEM((Z, GROUPS, rows, heads // GROUPS * vd), BF16),
             pltpu.VMEM((Z, 4, rows * columns // 128, 128), BF16),
             pltpu.VMEM((32, rows * columns // 128, 128), BF16),

time: 77.1 us -> 76 us (0.986)
  Pallas kernels: 75.5 us -> 74.4 us
    pallas_call x1, Pallas kernels: 75.5 us -> 74.4 us  [body(): pl.pallas_call(kernel, out_shape=jax.ShapeDtypeStruct((columns, 4 * rows)...]
where the time goes in v5:
time: 76 us; the launch traced here: 75.9 us
  Pallas kernels  74.4 us (98%)
  local copies, waits for them, and re-layouts  1.55 us (2%)
    pallas_call x1, Pallas kernels, body(): pl.pallas_call(kernel, out_shape=jax.ShapeDtypeStruct((columns, 4 * rows)...  74.4 us
    unnamed x1, local copies, waits for them, and re-layouts  1.55 us

profile of v5, /device:TPU:5, one launch (start us, length us, event | category | flops | bytes accessed | tf_op | source)
XLA Modules:
  0.0 75.9 jit_solution(14299330329748913076)
XLA Ops:
  0.0 74.4 %shard_map.73 = bf16[224,256]{1,0:T(8,128)(2,1)} custom-call(bf16[64,2048]{1,0:T(8,128)(2,1)} %qn_hbm.1, bf16[64,1024]{1,0:T(8,128)(2,1)} %qr_hbm.1, bf16[16,128,512]{2,1,0:T(8,128)(2,1)} %ka_hbm.1, bf16[16,512,128]{2,1,0:T(8,128)(2,1)} %va_hbm.1, bf16[224,2048]{1,0:T(8,128)(2,1)} %bitcast.2, bf16[512,128]{1,0:T(8,128)(2,1)} %lat_hbm.1, bf16[64,128]{1,0:T(8,128)(2,1)} %rk_hbm.1), custom_call_target="tpu_custom_call" | custom-call | tf_op jit(solution)/shard_map/pallas_call | solution.py:427
  74.4 1.6 %copy.9 = bf16[256,224]{0,1:T(8,128)(2,1)} copy(bf16[256,224]{0,1:T(8,128)(2,1)} %bitcast.3) | data formatting | bytes 229376

commit v6 on v5

--- a/solution.py
+++ b/solution.py
@@ -352,11 +352,10 @@
 
         lax.fori_loop(0, 4, one, 0)
 
-    pass_on(1, 0)
     w_sends[1].wait_recv()
     w_sends[2].wait_recv()
     project([z])
-    for group in range(1, GROUPS):
+    for group in range(GROUPS):
         pass_on(1, group)
     project([wrap_z(z - 1), wrap_z(z + 1)])
     for step in (2, 3):

time: 76 us -> 76.3 us (level)
  no operation moved by 1% of the time
where the time goes in v6:
time: 76.3 us; the launch traced here: 76.2 us
  Pallas kernels  74.7 us (98%)
  local copies, waits for them, and re-layouts  1.55 us (2%)
    pallas_call x1, Pallas kernels, body(): pl.pallas_call(kernel, out_shape=jax.ShapeDtypeStruct((columns, 4 * rows)...  74.7 us
    unnamed x1, local copies, waits for them, and re-layouts  1.55 us

profile of v6, /device:TPU:5, one launch (start us, length us, event | category | flops | bytes accessed | tf_op | source)
XLA Modules:
  0.0 76.2 jit_solution(16582060013448659340)
XLA Ops:
  0.0 74.7 %shard_map.73 = bf16[224,256]{1,0:T(8,128)(2,1)} custom-call(bf16[64,2048]{1,0:T(8,128)(2,1)} %qn_hbm.1, bf16[64,1024]{1,0:T(8,128)(2,1)} %qr_hbm.1, bf16[16,128,512]{2,1,0:T(8,128)(2,1)} %ka_hbm.1, bf16[16,512,128]{2,1,0:T(8,128)(2,1)} %va_hbm.1, bf16[224,2048]{1,0:T(8,128)(2,1)} %bitcast.2, bf16[512,128]{1,0:T(8,128)(2,1)} %lat_hbm.1, bf16[64,128]{1,0:T(8,128)(2,1)} %rk_hbm.1), custom_call_target="tpu_custom_call" | custom-call | tf_op jit(solution)/shard_map/pallas_call | solution.py:426
  74.7 1.6 %copy.9 = bf16[256,224]{0,1:T(8,128)(2,1)} copy(bf16[256,224]{0,1:T(8,128)(2,1)} %bitcast.3) | data formatting | bytes 229376
